TPU v7x, 256 devices: a whole 4x4x8 slice. The times are simulated.
256 devices in a mesh: sec: 64 (over z, x, y_hi), dof: 4 (over y_lo, core).
Axes of the slice: x: 4, y: 4 (y_hi: 2, y_lo: 2; y = y_hi * 2 + y_lo), z: 8, core: 2. Of those that a mesh axis runs over, the one named last changes fastest.
Arguments:
- sector_modes: bfloat16 [128, 32, 32768], P('sec', None, 'dof'), may hold values from -12 to 12
- tip_modes: bfloat16 [128, 64, 128], P('sec'), may hold values from -36 to 36
- tip_index: int32 [128, 128], replicated, may hold values from 0 to 32767
- nominal_eig: float32 [128, 32], P('sec'), may hold values from 0.5 to 2
- measured_eig: float32 [64], replicated, may hold values from 0.5 to 2
- pairing: int32 [64], replicated, may hold values from 0 to 31
Outputs:
- harmonic_modes: bfloat16 [128, 32, 32768], P('sec', None, 'dof')
- mac_values: float32 [128, 32, 64], P('sec')
- normal_matrix: float32 [128, 128], P('sec')
- normal_rhs: float32 [128], P('sec')
All inputs are finite; a program needn't handle non-finite values.
Results may differ from a plain program's by a relative error of at most 0.0069.
Values may be sent and summed in bfloat16 or wider, within the bound.
A program may use at most 128 MiB of HBM per device.

v0:
```python
import math

import jax
import jax.numpy as jnp
from jax import lax
from jax.sharding import PartitionSpec as P


def harmonic_table(row_count, sectors, first_row):
    row_ids = first_row + lax.broadcasted_iota(jnp.int32, (row_count, sectors), 0)
    sector_ids = lax.broadcasted_iota(jnp.int32, (row_count, sectors), 1)
    phase = row_ids * sector_ids % sectors
    angle = phase.astype(jnp.float32) * (2.0 * math.pi / sectors)
    scale = math.sqrt(2.0 / sectors)
    return jnp.where(row_ids <= sectors // 2, jnp.cos(angle), jnp.sin(angle)) * scale


def on_device(sector_modes, tip_modes, tip_index, nominal_eig, measured_eig, pairing):
    highest = lax.Precision.HIGHEST
    sec_count = lax.axis_size("sec")
    sec_rank = lax.axis_index("sec")
    local_sectors, families, dof_local = sector_modes.shape
    sectors = local_sectors * sec_count
    mode_count = tip_modes.shape[1]
    tip_count = tip_modes.shape[2]
    table_low = harmonic_table(sectors, sectors, 0).astype(jnp.bfloat16)
    table_mine = harmonic_table(local_sectors, sectors, sec_rank * local_sectors)
    spectral = jnp.einsum(
        "rs,sfd->rfd",
        table_low,
        lax.all_to_all(sector_modes, "sec", split_axis=2, concat_axis=0, tiled=True),
        preferred_element_type=jnp.float32,
    ).astype(jnp.bfloat16)
    harmonic = lax.all_to_all(spectral, "sec", split_axis=0, concat_axis=2, tiled=True)
    all_tips = lax.all_gather(tip_modes, "sec", axis=0, tiled=True)
    flat_index = tip_index.reshape(-1)
    whole = lax.all_gather(harmonic, "dof", axis=2, tiled=True)
    shaped = jnp.take(whole, flat_index, axis=2).reshape(
        local_sectors, families, sectors, tip_count
    )
    blocks = jnp.einsum("rfsp,smp->rsfm", shaped, all_tips, preferred_element_type=jnp.float32)
    projection = jnp.einsum("rs,rsfm->rfm", table_mine, blocks, precision=highest)
    weighted = shaped.astype(jnp.float32) * table_mine[:, None, :, None]
    projection, mode_power = (projection, jnp.sum(weighted * weighted, axis=(2, 3)))
    tip_wide = all_tips.astype(jnp.float32)
    tip_power = jnp.sum(tip_wide * tip_wide, axis=(0, 2))
    mac_values = (
        sectors
        * tip_count
        * projection
        * projection
        / ((mode_power[:, :, None] + 1e-06) * (tip_power[None, None, :] + 1e-06))
    )
    family_ids = lax.broadcasted_iota(jnp.int32, (families, mode_count), 0)
    paired = jnp.where(family_ids == pairing[None, :], 4.0, 0.0).astype(jnp.float32)
    weight = mac_values + paired[None, :, :]
    blade_part = jnp.einsum("rs,rfm->sfm", table_mine, projection, precision=highest)
    blade_amps = lax.psum(blade_part, "sec")
    target = (measured_eig[None, None, :] - nominal_eig[:, :, None]) * projection
    flat_amps = blade_amps.reshape(sectors, families * mode_count)
    right_term = table_mine[:, :, None] * flat_amps[None, :, :]
    left_term = right_term * weight.reshape(local_sectors, 1, families * mode_count)
    norm_factor = float(families * mode_count * tip_count)
    normal_part = jnp.einsum("rsk,rtk->st", left_term, right_term, precision=highest) / norm_factor
    rhs_part = (
        jnp.einsum(
            "rsk,rk->s",
            left_term,
            target.reshape(local_sectors, families * mode_count),
            precision=highest,
        )
        / norm_factor
    )
    normal_matrix, normal_rhs = (
        lax.psum_scatter(normal_part, "sec", scatter_dimension=0, tiled=True),
        lax.psum_scatter(rhs_part, "sec", scatter_dimension=0, tiled=True),
    )
    return (harmonic, mac_values, normal_matrix, normal_rhs)


def solution(mesh):
    return jax.shard_map(
        on_device,
        mesh=mesh,
        in_specs=(P("sec", None, "dof"), P("sec", None, None), P(), P("sec", None), P(), P()),
        out_specs=(P("sec", None, "dof"), P("sec", None, None), P("sec", None), P("sec")),
        check_vma=False,
    )
```

profile of v0, /device:TPU:22, one launch (start us, length us, event | category | flops | bytes accessed | tf_op | source)
XLA Modules:
  0.0 1714.4 jit_solution(11824156558476615684)
XLA Ops:
  7.2 9.2 copy.20
  16.3 9.8 reshape.204
  26.2 14.4 all-to-all-start
  41.4 27.3 %all-to-all-done = bf16[64,2,4096]{2,1,0:T(2,128)(2,1)S(1)} async-done(((bf16[64,2,4096]{2,1,0:T(2,128)(2,1)}), bf16[64,2,4096]{2,1,0:T(2,128)(2,1)S(1)}, u32[]{:S(2)}, u32[]{:S(2)}) %all-to-all-start) | async-done | bytes 1048608 | tf_op jit(solution)/shard_map/all_to_all | solution.py:31
  68.6 3.5 reshape.205
  72.1 9.6 copy.21
  83.1 36.7 %all_to_all.36 = bf16[128,32,128]{2,1,0:T(8,128)(2,1)S(1)} all-to-all(bf16[128,32,128]{2,1,0:T(8,128)(2,1)S(1)} %copy.22), channel_id=1, replica_groups=mesh['sec'=64,'dof'=4] {'sec'}, dimensions={0} | all-to-all | bytes 2097152 | tf_op jit(solution)/shard_map/all_to_all | solution.py:34
  123.0 40.2 %all-gather.5.cloned.1.call-done = bf16[128,64,128]{2,1,0:T(8,128)(2,1)} async-done(((bf16[2,64,128]{2,1,0:T(8,128)(2,1)}), bf16[128,64,128]{2,1,0:T(8,128)(2,1)}) %all-gather.5.cloned.1.call-update) | async-done | bytes 2097168 | tf_op jit(solution)/shard_map/all_gather | solution.py:35
  163.2 2.2 multiply_reduce_fusion.1
  165.4 47.7 %all-gather.3.cloned.1.call-done = bf16[2,32,32768]{2,1,0:T(8,128)(2,1)} async-done(((bf16[2,32,8192]{2,1,0:T(8,128)(2,1)}), bf16[2,32,32768]{2,1,0:T(8,128)(2,1)}) %all-gather.3.cloned.1.call-update) | async-done | bytes 4194320 | tf_op jit(solution)/shard_map/all_gather | solution.py:37
  213.1 33.1 %copy.24 = bf16[2,32,32768]{1,0,2:T(2,128)(2,1)} copy(bf16[2,32,32768]{2,1,0:T(8,128)(2,1)} %all-gather.3.cloned.1.call-done) | data formatting | bytes 8388608 | tf_op jit(solution)/shard_map/all_gather | solution.py:37
  246.2 111.8 %gather_fusion = bf16[16384,2,32]{2,1,0:T(2,128)(2,1)} fusion(bf16[2,32,32768]{1,0,2:T(2,128)(2,1)} %copy.24, s32[16384]{0:T(1024)S(1)} %broadcast_clamp_fusion), kind=kCustom, calls=%fused_computation | custom fusion | bytes 4259840 | tf_op jit(solution)/shard_map/jit(_take)/gather | solution.py:38
  358.0 15.7 copy.25
  373.7 2.8 convolution_bitcast_fusion
  376.5 4.3 fusion
  380.8 2.9 fusion.43
  384.6 58.3 %multiply_reduce_fusion = f32[2,32]{1,0:T(2,128)S(1)} fusion(f32[2,16384]{0,1:T(8,128)S(1)} %bitcast.58, bf16[16384,2,32]{2,1,0:T(2,128)(2,1)} %gather_fusion, pred[16384]{0:T(1024)(128)(4,1)S(1)} %compare_and_fusion), kind=kLoop, calls=%fused_computation.1 | loop fusion | flops 5242816 | bytes 2244864 | tf_op jit(solution)/shard_map/reduce_sum | solution.py:44
  443.8 628.0 %all-reduce.5.cloned.1.call-done = f32[128,2048]{0,1:T(8,128)} async-done(((f32[128,2048]{0,1:T(8,128)}), f32[128,2048]{0,1:T(8,128)}) %all-reduce.5.cloned.1.call-update) | async-done | bytes 1048592 | tf_op jit(solution)/shard_map/psum | solution.py:58
  1071.7 1.6 copy.28
  1073.3 2.7 fusion.16
  1076.0 1.8 fusion.24
  1077.9 176.0 %all-reduce.1 = f32[128]{0:T(128)S(1)} all-reduce(f32[128]{0:T(128)S(1)} %fusion.24), channel_id=3, replica_groups=mesh['sec'=64,'dof'=4] {'sec'}, use_global_device_ids=true, to_apply=%region_4.5.clone | all-reduce | flops 128 | bytes 1024
  1254.4 452.2 %all-reduce.7.cloned.1.call-done = f32[128,128]{1,0:T(8,128)} async-done(((f32[128,128]{1,0:T(8,128)}), f32[128,128]{1,0:T(8,128)}) %all-reduce.7.cloned.1.call-update) | async-done | bytes 65552
  1706.6 1.2 constant_dynamic-slice_fusion
  (39 shorter events, 6.8 us)
Async XLA Ops:
  26.2 42.4 %all-to-all-start = ((bf16[64,2,4096]{2,1,0:T(2,128)(2,1)}), bf16[64,2,4096]{2,1,0:T(2,128)(2,1)S(1)}, u32[]{:S(2)}, u32[]{:S(2)}) async-start(bf16[64,2,4096]{2,1,0:T(2,128)(2,1)} %reshape.204), calls=%async_computation | async-start | bytes 2097152 | tf_op jit(solution)/shard_map/all_to_all | solution.py:31
  40.6 122.7 %all-gather.5.cloned.1.call-start = ((), (), s32[]{:S(2)}) async-start(), calls=%async_computation.3 | async-start | bytes 2129920 | tf_op jit(solution)/shard_map/all_gather | solution.py:35
  41.3 171.8 %all-gather.3.cloned.1.call-start = ((), (), s32[]{:S(2)}) async-start(), calls=%async_computation.2 | async-start | bytes 5242880 | tf_op jit(solution)/shard_map/all_gather | solution.py:37
  119.9 1.7 copy-start.4
  119.9 2.9 copy-start.3
  119.9 3.0 copy-start
  121.1 950.7 %all-reduce.5.cloned.1.call-start = ((), (), s32[]{:S(2)}) async-start(), calls=%async_computation.4 | async-start | bytes 2097152 | tf_op jit(solution)/shard_map/psum | solution.py:58
  383.7 1322.9 %all-reduce.7.cloned.1.call-start = ((), (), s32[]{:S(2)}) async-start(), calls=%async_computation.5 | async-start | bytes 131072
  384.5 58.3 %copy-start.1 = (f32[2,32]{1,0:T(2,128)S(1)}, f32[2,32]{1,0:T(2,128)}, u32[]{:S(2)}) copy-start(f32[2,32]{1,0:T(2,128)} %param.9) | copy-start | bytes 772
  384.6 58.3 %copy-start.2 = (f32[64]{0:T(128)S(1)}, f32[64]{0:T(128)}, u32[]{:S(2)}) copy-start(f32[64]{0:T(128)} %param.10) | copy-start | bytes 772
Sparse Core Ops, SparseCore 0:
  44.9 118.2 all-gather.4
  165.6 47.4 all-gather.2
  383.8 687.8 all-reduce.4
  1076.2 630.4 all-reduce.6
where the time goes:
time: 1720 us; the launch traced here: 1710 us
  waiting for transfers between devices  1200 us (70%)
  blocking collectives  213 us (12%)
  local copies, waits for them, and re-layouts  199 us (12%)
  other arithmetic  61.4 us (4%)
    psum x1, waiting for transfers between devices, on_device(): blade_amps = lax.psum(blade_part, 'sec')  628 us
    unnamed x5, waiting for transfers between devices  453 us
    unnamed x1, blocking collectives  176 us
    gather x2, local copies, waits for them, and re-layouts, on_device(): jnp.take(whole, flat_index, axis=2)  127 us
    reduce_sum x1, other arithmetic, on_device(): jnp.sum(weighted * weighted, axis=(2, 3))  58.3 us
    all_gather x1, waiting for transfers between devices, on_device(): whole = lax.all_gather(harmonic, 'dof', axis=2, tiled=True)  47.7 us
    all_gather x1, waiting for transfers between devices, on_device(): all_tips = lax.all_gather(tip_modes, 'sec', axis=0, tiled=True)  40.2 us
    all_to_all x1, blocking collectives, on_device(): lax.all_to_all(spectral, 'sec', split_axis=0, concat_axis=2, tiled=True)  36.7 us
  transfers between devices with their start and end apart: 5, of which 5 were waited for; matrix products, arithmetic and copies ran while one was open for 5% of the time, Pallas kernels for 0%

commit v1 on v0

v1 whole, which is shorter than its diff:
```python
import functools
import math

import jax
import jax.numpy as jnp
from jax import lax
from jax.experimental import pallas as pl
from jax.experimental.pallas import tpu as pltpu
from jax.sharding import PartitionSpec as P

MESH = pl.DeviceIdType.MESH


def harmonic_table(row_count, sectors, first_row):
    row_ids = first_row + lax.broadcasted_iota(jnp.int32, (row_count, sectors), 0)
    sector_ids = lax.broadcasted_iota(jnp.int32, (row_count, sectors), 1)
    phase = row_ids * sector_ids % sectors
    angle = phase.astype(jnp.float32) * (2.0 * math.pi / sectors)
    scale = math.sqrt(2.0 / sectors)
    return jnp.where(row_ids <= sectors // 2, jnp.cos(angle), jnp.sin(angle)) * scale


def transform_kernel(n, x_ref, table_ref, out_ref, mid_ref, recv, wide, done, ssem, rsem, lsem):
    me, q = lax.axis_index("sec"), lax.axis_index("dof")
    own = x_ref.shape[0]
    chunks, sectors, rows, lanes = recv.shape

    barrier = pltpu.get_barrier_semaphore()

    def greet(k, c):
        pl.semaphore_signal(barrier, inc=1, device_id=(me ^ k, q), device_id_type=MESH)
        return c

    lax.fori_loop(1, n, greet, 0)
    pl.semaphore_wait(barrier, n - 1)

    def columns(j):
        return pl.ds(pl.multiple_of(lanes * j, lanes), lanes)

    def mine(j):
        return pl.ds(own * j, own)

    for h in range(chunks):
        family = pl.ds(rows * h, rows)

        def send(k, c, h=h, family=family):
            j = me ^ k
            pltpu.make_async_remote_copy(
                src_ref=x_ref.at[:, family, columns(j)],
                dst_ref=recv.at[h, mine(me)],
                send_sem=ssem.at[h],
                recv_sem=rsem.at[h],
                device_id=(j, q),
                device_id_type=MESH,
            ).start()
            return c

        lax.fori_loop(1, n, send, 0)
        pltpu.make_async_copy(x_ref.at[:, family, columns(me)], recv.at[h, mine(me)], lsem.at[h]).start()

    for h in range(chunks):
        family = pl.ds(rows * h, rows)
        others = recv.at[h, pl.ds(0, own * (n - 1))]
        pltpu.make_async_remote_copy(
            src_ref=others, dst_ref=others, send_sem=ssem.at[h], recv_sem=rsem.at[h],
            device_id=(me, q), device_id_type=MESH,
        ).wait_recv()
        pltpu.make_async_copy(recv.at[h, mine(me)], recv.at[h, mine(me)], lsem.at[h]).wait()
        wide[...] = recv[h].reshape(sectors * rows, lanes).astype(jnp.float32)
        table = table_ref[...]
        for f in range(0, rows, 2):
            pair = [wide[pl.ds(f + i, sectors, stride=rows), :] for i in range(2)]
            both = jnp.concatenate(pair, axis=1).astype(jnp.bfloat16)
            result = jnp.dot(table, both, preferred_element_type=jnp.float32)
            for i in range(2):
                done[pl.ds(f + i, sectors, stride=rows), :] = result[:, lanes * i:lanes * (i + 1)]
        mid_ref[h] = done[...].reshape(sectors, rows, lanes).astype(jnp.bfloat16)

        def back(k, c, h=h, family=family):
            j = me ^ k
            pltpu.make_async_remote_copy(
                src_ref=mid_ref.at[h, mine(j)],
                dst_ref=out_ref.at[:, family, columns(me)],
                send_sem=ssem.at[chunks + h],
                recv_sem=rsem.at[chunks + h],
                device_id=(j, q),
                device_id_type=MESH,
            ).start()
            return c

        lax.fori_loop(1, n, back, 0)
        pltpu.make_async_copy(mid_ref.at[h, mine(me)], out_ref.at[:, family, columns(me)], lsem.at[chunks + h]).start()

    for h in range(chunks):
        others = recv.at[h, pl.ds(0, own * (n - 1))]
        first = pltpu.make_async_remote_copy(
            src_ref=others, dst_ref=others, send_sem=ssem.at[h], recv_sem=rsem.at[h],
            device_id=(me, q), device_id_type=MESH,
        )
        first.wait_send()
        target = out_ref.at[:, pl.ds(rows * h, rows), pl.ds(0, lanes * (n - 1))]
        second = pltpu.make_async_remote_copy(
            src_ref=target, dst_ref=target, send_sem=ssem.at[chunks + h], recv_sem=rsem.at[chunks + h],
            device_id=(me, q), device_id_type=MESH,
        )
        second.wait_recv()
        second.wait_send()
        local = out_ref.at[:, pl.ds(rows * h, rows), pl.ds(0, lanes)]
        pltpu.make_async_copy(local, local, lsem.at[chunks + h]).wait()


def transform(sector_modes, table_low, n):
    own, families, dof_local = sector_modes.shape
    sectors = own * n
    lanes = dof_local // n
    chunks = 2
    rows = families // chunks
    vmem = pl.BlockSpec(memory_space=pltpu.VMEM)
    return pl.pallas_call(
        functools.partial(transform_kernel, n),
        out_shape=(
            jax.ShapeDtypeStruct((own, families, dof_local), jnp.bfloat16),
            jax.ShapeDtypeStruct((chunks, sectors, rows, lanes), jnp.bfloat16),
        ),
        in_specs=[vmem, vmem],
        out_specs=(pl.BlockSpec(memory_space=pl.ANY), vmem),
        scratch_shapes=[
            pltpu.VMEM((chunks, sectors, rows, lanes), jnp.bfloat16),
            pltpu.VMEM((sectors * rows, lanes), jnp.float32),
            pltpu.VMEM((sectors * rows, lanes), jnp.float32),
            pltpu.SemaphoreType.DMA((2 * chunks,)),
            pltpu.SemaphoreType.DMA((2 * chunks,)),
            pltpu.SemaphoreType.DMA((2 * chunks,)),
        ],
        compiler_params=pltpu.CompilerParams(
            collective_id=0, has_side_effects=True, vmem_limit_bytes=48 * 2**20
        ),
        name="transform",
    )(sector_modes, table_low)


def on_device(sector_modes, tip_modes, tip_index, nominal_eig, measured_eig, pairing):
    highest = lax.Precision.HIGHEST
    n = lax.axis_size("sec")
    me, q = lax.axis_index("sec"), lax.axis_index("dof")
    local_sectors, families, dof_local = sector_modes.shape
    sectors = local_sectors * n
    mode_count, tip_count = tip_modes.shape[1:]
    lanes = dof_local // n
    table = harmonic_table(sectors, sectors, 0)
    table_mine = harmonic_table(local_sectors, sectors, me * local_sectors)
    harmonic, mid = transform(sector_modes, table.astype(jnp.bfloat16), n)
    mid = mid.transpose(1, 0, 2, 3).reshape(sectors, families, lanes)
    all_tips = lax.all_gather(tip_modes, "sec", axis=0, tiled=True)
    first = q * dof_local + me * lanes
    chosen = tip_index[:, None, :] == first + lax.broadcasted_iota(jnp.int32, (1, lanes, 1), 1)
    chosen = chosen.astype(jnp.bfloat16)
    spread = jnp.einsum("sdp,smp->smd", chosen, all_tips, preferred_element_type=jnp.float32)
    gather = jnp.einsum("rs,smd->rmd", table, spread, precision=highest)
    part = jnp.einsum("rfd,rmd->rfm", mid.astype(jnp.float32), gather, precision=highest)
    counts = jnp.sum(chosen.astype(jnp.float32), axis=2)
    power = jnp.dot(table * table, counts, precision=highest)
    mid_wide = mid.astype(jnp.float32)
    power_part = jnp.einsum("rfd,rd->rf", mid_wide * mid_wide, power, precision=highest)
    both = lax.psum(jnp.concatenate([part, power_part[:, :, None]], axis=2), ("sec", "dof"))
    full = both[:, :, :mode_count]
    projection = lax.dynamic_slice_in_dim(full, me * local_sectors, local_sectors, 0)
    mode_power = lax.dynamic_slice_in_dim(both[:, :, mode_count], me * local_sectors, local_sectors, 0)
    tip_wide = all_tips.astype(jnp.float32)
    tip_power = jnp.sum(tip_wide * tip_wide, axis=(0, 2))
    mac_values = (
        sectors * tip_count * projection * projection
        / ((mode_power[:, :, None] + 1e-06) * (tip_power[None, None, :] + 1e-06))
    )
    family_ids = lax.broadcasted_iota(jnp.int32, (families, mode_count), 0)
    paired = jnp.where(family_ids == pairing[None, :], 4.0, 0.0).astype(jnp.float32)
    weight = mac_values + paired[None, :, :]
    blade_amps = jnp.einsum("rs,rfm->sfm", table, full, precision=highest)
    target = (measured_eig[None, None, :] - nominal_eig[:, :, None]) * projection
    flat_amps = blade_amps.reshape(sectors, families * mode_count)
    right_term = table_mine[:, :, None] * flat_amps[None, :, :]
    left_term = right_term * weight.reshape(local_sectors, 1, families * mode_count)
    norm_factor = float(families * mode_count * tip_count)
    normal_part = jnp.einsum("rsk,rtk->st", left_term, right_term, precision=highest) / norm_factor
    rhs_part = (
        jnp.einsum(
            "rsk,rk->s",
            left_term,
            target.reshape(local_sectors, families * mode_count),
            precision=highest,
        )
        / norm_factor
    )
    normal_matrix, normal_rhs = (
        lax.psum_scatter(normal_part, "sec", scatter_dimension=0, tiled=True),
        lax.psum_scatter(rhs_part, "sec", scatter_dimension=0, tiled=True),
    )
    return (harmonic, mac_values, normal_matrix, normal_rhs)


def solution(mesh):
    return jax.shard_map(
        on_device,
        mesh=mesh,
        in_specs=(P("sec", None, "dof"), P("sec", None, None), P(), P("sec", None), P(), P()),
        out_specs=(P("sec", None, "dof"), P("sec", None, None), P("sec", None), P("sec")),
        check_vma=False,
    )
```

time: 1720 us -> 1060 us (0.62)
  waiting for transfers between devices: 1200 us -> 773 us
  local copies, waits for them, and re-layouts: 199 us -> 9.63 us
  Pallas kernels: 0 us -> 60.3 us
  other arithmetic: 61.4 us -> 4.99 us
  blocking collectives: 213 us -> 165 us
    psum x1, waiting for transfers between devices: 628 us -> 258 us  [on_device(): lax.psum(jnp.concatenate([part, power_part[:, :, None]], axis=2), ('sec',...]
    gather x2 -> x0, local copies, waits for them, and re-layouts: 127 us -> none  [on_device(): jnp.take(whole, flat_index, axis=2)]
    pallas_call x0 -> x1, Pallas kernels: none -> 60.3 us  [transform(): pl.pallas_call(functools.partial(transform_kernel, n), out_shape=(jax.Sha...]
    reduce_sum x1, other arithmetic: 58.3 us -> 1.26 us  [on_device(): counts = jnp.sum(chosen.astype(jnp.float32), axis=2)]
    all_gather x1 -> x0, waiting for transfers between devices: 47.7 us -> none  [on_device(): whole = lax.all_gather(harmonic, 'dof', axis=2, tiled=True)]
    all_to_all x1 -> x0, blocking collectives: 36.7 us -> none  [on_device(): lax.all_to_all(spectral, 'sec', split_axis=0, concat_axis=2, tiled=True)]
    all_gather x1 -> x0, local copies, waits for them, and re-layouts: 33.1 us -> none  [on_device(): whole = lax.all_gather(harmonic, 'dof', axis=2, tiled=True)]
    all_to_all x1 -> x0, waiting for transfers between devices: 27.3 us -> none  [on_device(): lax.all_to_all(sector_modes, 'sec', split_axis=2, concat_axis=0, tiled=True)]
  transfers between devices with their start and end apart: 5 -> 3, of which waited for: 5 -> 3; matrix products, arithmetic and copies ran while one was open for 5% -> 1% of each run, Pallas kernels for 0% -> 6%
where the time goes in v1:
time: 1060 us
  waiting for transfers between devices  773 us (73%)
  blocking collectives  165 us (16%)
  Pallas kernels  60.3 us (6%)
  matrix products  27.6 us (3%)
  between operations  14.6 us (1%)
    unnamed x4, waiting for transfers between devices  455 us
    psum x1, waiting for transfers between devices, on_device(): lax.psum(jnp.concatenate([part, power_part[:, :, None]], axis=2), ('sec',...  258 us
    unnamed x1, blocking collectives  165 us
    all_gather x1, waiting for transfers between devices, on_device(): all_tips = lax.all_gather(tip_modes, 'sec', axis=0, tiled=True)  60.3 us
    pallas_call x1, Pallas kernels, transform(): pl.pallas_call(functools.partial(transform_kernel, n), out_shape=(jax.Sha...  60.3 us
  transfers between devices with their start and end apart: 3, of which 3 were waited for; matrix products, arithmetic and copies ran while one was open for 1% of the time, Pallas kernels for 6%

profile of v1, /device:TPU:22, one launch (start us, length us, event | category | flops | bytes accessed | tf_op | source)
XLA Modules:
  0.0 1055.7 jit_solution(10632286906476239852)
XLA Ops:
  7.2 0.7 all-gather.2.cloned.1.call-update
  8.3 1.2 copy-done
  9.5 60.3 %transform.1 = (bf16[2,32,8192]{2,1,0:T(8,128)(2,1)S(1)}, bf16[2,128,16,128]{3,2,1,0:T(8,128)(2,1)S(1)}) custom-call(bf16[2,32,8192]{2,1,0:T(8,128)(2,1)S(1)} %copy-done, bf16[128,128]{1,0:T(8,128)(2,1)S(1)} %fusion.56.table_ref), custom_call_target="tpu_custom_call" | custom-call | tf_op jit(solution)/shard_map/transform/pallas_call | solution.py:119
  70.0 1.3 convert_reduce_fusion
  71.8 3.3 fusion.20
  75.1 60.3 %all-gather.2.cloned.1.call-done = bf16[128,64,128]{2,1,0:T(8,128)(2,1)} async-done(((bf16[2,64,128]{2,1,0:T(8,128)(2,1)}), bf16[128,64,128]{2,1,0:T(8,128)(2,1)}) %all-gather.2.cloned.1.call-update) | async-done | bytes 2097168 | tf_op jit(solution)/shard_map/all_gather | solution.py:154
  135.4 4.7 fusion.14
  140.1 6.3 fusion.4
  146.4 5.8 fusion.2
  152.2 1.9 pad_maximum_fusion
  154.8 0.6 dynamic-slice.1
  156.0 0.6 multiply_reduce_fusion
  156.6 257.9 %all-reduce.5.cloned.1.call-done = f32[128,32,65]{2,1,0:T(8,128)} async-done(((f32[128,32,65]{2,1,0:T(8,128)}), f32[128,32,65]{2,1,0:T(8,128)}) %all-reduce.5.cloned.1.call-update) | async-done | bytes 1064976 | tf_op jit(solution)/shard_map/psum | solution.py:165
  414.5 3.8 copy.20
  418.3 0.6 slice.9
  419.0 0.7 broadcast_add_fusion
  419.9 2.6 fusion.55
  422.4 2.8 fusion.28
  425.2 1.8 fusion.36
  427.1 165.0 %all-reduce.1 = f32[128]{0:T(128)S(1)} all-reduce(f32[128]{0:T(128)S(1)} %fusion.36), channel_id=3, replica_groups=mesh['sec'=64,'dof'=4] {'sec'}, use_global_device_ids=true, to_apply=%region_4.5.clone | all-reduce | flops 128 | bytes 1024
  592.0 0.6 dynamic-slice.4
  592.6 454.3 %all-reduce.7.cloned.1.call-done = f32[128,128]{1,0:T(8,128)} async-done(((f32[128,128]{1,0:T(8,128)}), f32[128,128]{1,0:T(8,128)}) %all-reduce.7.cloned.1.call-update) | async-done | bytes 65552
  1046.9 1.2 constant_dynamic-slice_fusion
  1048.2 1.0 copy.32
  (35 shorter events, 2.0 us)
Async XLA Ops:
  7.2 62.8 %copy-start.4 = (s32[128,128]{1,0:T(8,128)S(1)}, s32[128,128]{1,0:T(8,128)}, u32[]{:S(2)}) copy-start(s32[128,128]{1,0:T(8,128)} %param.8) | copy-start | bytes 196612
  7.2 64.1 %copy-start.7 = (s32[64]{0:T(128)S(1)}, s32[64]{0:T(128)}, u32[]{:S(2)}) copy-start(s32[64]{0:T(128)} %param.11) | copy-start | bytes 772
  7.2 128.2 %all-gather.2.cloned.1.call-start = ((), (), s32[]{:S(2)}) async-start(), calls=%async_computation | async-start | bytes 2129920 | tf_op jit(solution)/shard_map/all_gather | solution.py:154
  7.9 406.6 %all-reduce.5.cloned.1.call-start = ((), (), s32[]{:S(2)}) async-start(), calls=%async_computation.1 | async-start | bytes 4194304 | tf_op jit(solution)/shard_map/psum | solution.py:165
  8.3 1.2 copy-start
  146.4 5.8 copy-start.3
  154.1 0.7 copy-start.8
  154.1 1.9 copy-start.2
  154.1 892.8 %all-reduce.7.cloned.1.call-start = ((), (), s32[]{:S(2)}) async-start(), calls=%async_computation.2 | async-start | bytes 131072
  414.5 3.8 copy-start.1
  418.3 0.7 copy-start.5
  418.3 0.7 copy-start.6
Sparse Core Ops, SparseCore 0:
  11.5 123.8 all-gather.1
  154.2 260.1 all-reduce.4
  425.4 621.5 all-reduce.6

commit v2 on v0

v2 whole, which is shorter than its diff:
```python
import math

import jax
import jax.numpy as jnp
import numpy as np
from jax import lax
from jax.experimental import pallas as pl
from jax.experimental.pallas import tpu as pltpu
from jax.sharding import PartitionSpec as P

MESH = pl.DeviceIdType.MESH
HIGHEST = lax.Precision.HIGHEST
F32 = jnp.float32
BF16 = jnp.bfloat16
NT = (((1,), (1,)), ((), ()))

SECTORS, FAM, MODES, TIPS, LANES = 128, 32, 64, 128, 128
SEC, DOFS = 64, 4
NZ, NX, NY, NXY = 8, 4, 2, 8
CHUNKS = 2
ROWS = FAM // CHUNKS
HROWS = MODES + 8
QF = FAM // DOFS
STAGES = (
    "in0", "in1", "out0", "out1", "tip_z", "tip_x", "tip_y", "tip_core", "core", "lo",
    "xy", "z", "all_z", "all_xy", "mac", "nz", "nxy", "ndof",
)
STAGE = {name: i for i, name in enumerate(STAGES)}


def tables():
    rows, cols = np.meshgrid(np.arange(SECTORS), np.arange(SECTORS), indexing="ij")
    angle = 2.0 * np.pi * (rows * cols % SECTORS) / SECTORS
    table = math.sqrt(2.0 / SECTORS) * np.where(rows <= SECTORS // 2, np.cos(angle), np.sin(angle))
    table = table.astype(np.float32)

    def split(a):
        high = a.astype(BF16)
        low = (a - high.astype(np.float32)).astype(BF16)
        return np.concatenate([high, low], axis=1)

    xy, z = np.meshgrid(np.arange(NXY), np.arange(NZ), indexing="ij")
    order = (z * NXY + xy).reshape(-1)
    back = np.concatenate([table[2 * order].T, table[2 * order + 1].T], axis=0)
    return table, table.astype(BF16), split(table), split(table * table), back


def body(
    x_ref, tips_ref, index_ref, nominal_ref, measured_ref, pairing_ref,
    table_ref, low_ref, split_ref, square_ref, back_ref,
    out_ref, mac_ref, normal_ref, rhs_ref,
    recv, wide, done, mid, tips, spread, gather, power,
    part, from_core, half, from_lo, mine_xy, from_xy, mine_z, from_z, every, macs,
    n_z, n_from_z, n_xy, n_from_xy, n_dof, ssem, rsem, lsem,
):
    me, q = lax.axis_index("sec"), lax.axis_index("dof")
    z, x, y = me // NXY, (me // NY) % NX, me % NY
    xy = me % NXY
    lo, core = q // 2, q % 2
    quarter = 2 * core + lo

    barrier = pltpu.get_barrier_semaphore()

    def greet(k, c):
        pl.semaphore_signal(barrier, inc=1, device_id=(me ^ k, q), device_id_type=MESH)
        return c

    lax.fori_loop(1, SEC, greet, 0)
    for k in (1, 2, 3):
        pl.semaphore_signal(barrier, inc=1, device_id=(me, q ^ k), device_id_type=MESH)
    pl.semaphore_signal(barrier, inc=1, device_id=(me ^ 1, q ^ 2), device_id_type=MESH)

    def push(stage, src, dst, sec, dof):
        pltpu.make_async_remote_copy(
            src_ref=src, dst_ref=dst, send_sem=ssem.at[STAGE[stage]], recv_sem=rsem.at[STAGE[stage]],
            device_id=(sec, dof), device_id_type=MESH,
        ).start()

    def total(stage, ref):
        return pltpu.make_async_remote_copy(
            src_ref=ref, dst_ref=ref, send_sem=ssem.at[STAGE[stage]], recv_sem=rsem.at[STAGE[stage]],
            device_id=(me, q), device_id_type=MESH,
        )

    sent = []

    def arrived(stage, ref):
        total(stage, ref).wait_recv()
        sent.append((stage, ref))

    def columns(j):
        return pl.ds(pl.multiple_of(LANES * j, LANES), LANES)

    def mine(j):
        return pl.ds(2 * j, 2)

    def send_in(h):
        family = pl.ds(ROWS * h, ROWS)

        def step(k, c):
            j = me ^ k
            push(f"in{h}", x_ref.at[:, family, columns(j)], recv.at[h, mine(me)], j, q)
            return c

        lax.fori_loop(1, SEC, step, 0)
        pltpu.make_async_copy(x_ref.at[:, family, columns(me)], recv.at[h, mine(me)], lsem.at[h]).start()

    def transform(h):
        arrived(f"in{h}", recv.at[h, pl.ds(0, 2 * (SEC - 1))])
        pltpu.make_async_copy(recv.at[h, mine(me)], recv.at[h, mine(me)], lsem.at[h]).wait()
        wide[...] = recv[h].reshape(SECTORS * ROWS, LANES).astype(F32)
        table = low_ref[...]
        for f in range(0, ROWS, 2):
            pair = [wide[pl.ds(f + i, SECTORS, stride=ROWS), :] for i in range(2)]
            both = jnp.concatenate(pair, axis=1).astype(BF16)
            result = jnp.dot(table, both, preferred_element_type=F32)
            for i in range(2):
                done[pl.ds(f + i, SECTORS, stride=ROWS), :] = result[:, LANES * i:LANES * (i + 1)]
        mid[h] = done[...].reshape(SECTORS, ROWS, LANES).astype(BF16)

    def send_out(h):
        family = pl.ds(ROWS * h, ROWS)

        def step(k, c):
            j = me ^ k
            push(f"out{h}", mid.at[h, mine(j)], out_ref.at[:, family, columns(me)], j, q)
            return c

        lax.fori_loop(1, SEC, step, 0)
        pltpu.make_async_copy(mid.at[h, mine(me)], out_ref.at[:, family, columns(me)], lsem.at[CHUNKS + h]).start()

    own_y = pl.ds(2 * y, 2)
    tips[core, z, x, own_y] = tips_ref[:, pl.ds(pl.multiple_of(32 * core, 32), 32), :]
    pl.semaphore_wait(barrier, SEC + 3)
    for k in range(1, NZ):
        push("tip_z", tips.at[core, z, x, own_y], tips.at[core, z, x, own_y], me ^ (NXY * k), q)
    send_in(0)
    arrived("tip_z", tips.at[core, pl.ds(0, NZ - 1), 0, pl.ds(0, 2)])
    for k in range(1, NX):
        push("tip_x", tips.at[core, :, x, own_y], tips.at[core, :, x, own_y], me ^ (NY * k), q)
    send_in(1)
    arrived("tip_x", tips.at[core, :, pl.ds(0, NX - 1), pl.ds(0, 2)])
    push("tip_y", tips.at[core, :, :, own_y], tips.at[core, :, :, own_y], me ^ 1, q ^ 2)
    transform(0)
    send_out(0)
    arrived("tip_y", tips.at[core, :, :, pl.ds(0, 2)])
    push("tip_core", tips.at[core], tips.at[core], me, q ^ 1)
    transform(1)
    send_out(1)
    arrived("tip_core", tips.at[core])

    first = q * (SEC * LANES) + me * LANES
    column_ids = first + lax.broadcasted_iota(jnp.int32, (LANES, TIPS), 0)
    ones = jnp.ones((16, TIPS), BF16)

    def spread_step(s, tip_sum):
        one = [tips[c, s // 16, (s // 4) % 4, s % 4] for c in range(2)]
        block = jnp.concatenate(one + [ones], axis=0)
        chosen = jnp.where(index_ref[pl.ds(s, 1), :] == column_ids, 1.0, 0.0).astype(BF16)
        result = lax.dot_general(block, chosen, NT, preferred_element_type=F32)
        spread[pl.ds(pl.multiple_of(s * HROWS, 8), HROWS), :] = result[:HROWS]
        both = jnp.concatenate(one, axis=0).astype(F32)
        return tip_sum + both * both

    tip_sum = lax.fori_loop(0, SECTORS, spread_step, jnp.zeros((MODES, TIPS), F32), unroll=4)

    def twice(a):
        low = a.astype(BF16)
        return jnp.concatenate([low, low], axis=0)

    for m in range(0, MODES, 2):
        pair = [spread[pl.ds(m + i, SECTORS, stride=HROWS), :] for i in range(2)]
        both = twice(jnp.concatenate(pair, axis=1))
        result = jnp.dot(split_ref[...], both, preferred_element_type=F32)
        for i in range(2):
            gather[pl.ds(m + i, SECTORS, stride=MODES), :] = result[:, LANES * i:LANES * (i + 1)]
    counts = spread[pl.ds(MODES, SECTORS, stride=HROWS), :]
    power[...] = jnp.dot(square_ref[...], twice(counts), preferred_element_type=F32)

    lane_ids = lax.broadcasted_iota(jnp.int32, (FAM, LANES), 1)

    def project_step(j, mode_power):
        cols, squares = [], []
        for l in range(2):
            r = 2 * j + l
            rows = jnp.concatenate([mid[h, r] for h in range(CHUNKS)], axis=0)
            cols.append(rows)
            rows = rows.astype(F32)
            share = jnp.sum(rows * rows * power[pl.ds(r, 1), :], axis=1, keepdims=True)
            mode_power = jnp.where(lane_ids == r, share, mode_power)
        rows = jnp.concatenate(cols, axis=0)
        g = gather[pl.ds(pl.multiple_of(j * LANES, LANES), LANES), :]
        high = g.astype(BF16)
        low = (g - high.astype(F32)).astype(BF16)
        both = lax.dot_general(
            jnp.concatenate([rows, rows], axis=1), jnp.concatenate([high, low], axis=1), NT,
            preferred_element_type=F32,
        )
        pair = jnp.where(lane_ids < MODES, both[:FAM], both[FAM:])
        part[:, (j % NXY) * NZ + j // NXY] = pair.reshape(DOFS, QF, LANES)
        return mode_power

    mode_power = lax.fori_loop(0, SEC, project_step, jnp.zeros((FAM, LANES), F32), unroll=2)
    part[:, SEC] = mode_power.reshape(DOFS, QF, LANES)

    push("core", part.at[pl.ds(2 * (1 - core), 2)], from_core, me, q ^ 1)
    arrived("core", from_core)
    half[...] = part[pl.ds(2 * core, 2)] + from_core[...]
    push("lo", half.at[1 - lo], from_lo, me, q ^ 2)
    arrived("lo", from_lo)
    for i in range(NXY):
        mine_xy[i, pl.ds(0, NZ)] = half[lo, pl.ds(NZ * i, NZ)] + from_lo[pl.ds(NZ * i, NZ)]
        mine_xy[i, NZ] = half[lo, SEC] + from_lo[SEC]

    for k in range(1, NXY):
        push("xy", mine_xy.at[xy ^ k], from_xy.at[xy], me ^ k, q)
    from_xy[xy] = mine_xy[xy]
    arrived("xy", from_xy.at[pl.ds(0, NXY - 1)])
    columns_sum = jnp.sum(from_xy[...], axis=0)
    mine_z[:, 0] = columns_sum[:NZ]
    for i in range(NZ):
        mine_z[i, 1] = columns_sum[NZ]
    for k in range(1, NZ):
        push("z", mine_z.at[z ^ k], from_z.at[z], me ^ (NXY * k), q)
    from_z[z] = mine_z[z]
    arrived("z", from_z.at[pl.ds(0, NZ - 1)])
    whole = jnp.sum(from_z[...], axis=0)
    projection, mode_power = whole[0], whole[1]

    every[xy, z] = projection
    for k in range(1, NZ):
        push("all_z", every.at[xy, z], every.at[xy, z], me ^ (NXY * k), q)

    lane = lax.broadcasted_iota(jnp.int32, (QF, LANES), 1)
    row = lax.broadcasted_iota(jnp.int32, (QF, LANES), 0)

    def by_half(a, b):
        return jnp.where(lane < MODES, a, b)

    own_power = by_half(*[
        jnp.sum(jnp.where(lane == 2 * me + l, mode_power, 0.0), axis=1, keepdims=True) for l in range(2)
    ])
    tip_column = jnp.sum(tip_sum, axis=1, keepdims=True)
    mode_row = lax.broadcasted_iota(jnp.int32, (MODES, LANES), 0)
    mode_lane = lax.broadcasted_iota(jnp.int32, (MODES, LANES), 1) % MODES
    tip_power = jnp.sum(jnp.where(mode_row == mode_lane, tip_column, 0.0), axis=0, keepdims=True)
    mac = (SECTORS * TIPS) * projection * projection / ((own_power + 1e-06) * (tip_power + 1e-06))
    macs[quarter] = mac
    for k in (1, 2, 3):
        push("mac", macs.at[quarter], macs.at[quarter], me, q ^ k)
    family = QF * quarter + row
    pairing = jnp.concatenate([pairing_ref[...]] * 2, axis=1)
    weight = mac + jnp.where(family == pairing, 4.0, 0.0)
    measured = jnp.concatenate([measured_ref[...]] * 2, axis=1)
    nominal_row = lax.broadcasted_iota(jnp.int32, (QF, FAM), 0) + QF * quarter
    nominal_lane = lax.broadcasted_iota(jnp.int32, (QF, FAM), 1)
    nominal = by_half(*[
        jnp.sum(jnp.where(nominal_row == nominal_lane, nominal_ref[pl.ds(l, 1), :], 0.0), axis=1, keepdims=True)
        for l in range(2)
    ])
    pull = weight * ((measured - nominal) * projection)

    arrived("all_z", every.at[0, pl.ds(0, NZ - 1)])
    for k in range(1, NXY):
        push("all_xy", every.at[xy], every.at[xy], me ^ k, q)
    arrived("all_xy", every.at[pl.ds(0, NXY - 1)])

    flat = every.reshape(SEC * QF, LANES)
    amps = []
    for f in range(QF):
        both = jnp.dot(
            back_ref[...], flat[pl.ds(f, SEC, stride=QF), :], precision=HIGHEST, preferred_element_type=F32
        )
        amps.append(both[:SECTORS, :MODES] + both[SECTORS:, MODES:])
    square = lax.broadcasted_iota(jnp.int32, (SECTORS, SECTORS), 0) == lax.broadcasted_iota(
        jnp.int32, (SECTORS, SECTORS), 1
    )
    amps = [jnp.concatenate(amps[f:f + 2], axis=1) for f in range(0, QF, 2)]
    normal = jnp.zeros((SECTORS, SECTORS), F32)
    rhs = jnp.zeros((8, SECTORS), F32)
    for l in range(2):
        table_row = table_ref[pl.ds(2 * me + l, 1), :]
        table_column = jnp.sum(jnp.where(square, table_row, 0.0), axis=1, keepdims=True)
        inner = jnp.zeros((SECTORS, SECTORS), F32)
        inner_rhs = jnp.zeros((8, SECTORS), F32)
        for t in range(QF // 2):
            def flat_row(a, t=t, l=l):
                return jnp.concatenate(
                    [a[2 * t + i:2 * t + i + 1, MODES * l:MODES * (l + 1)] for i in range(2)], axis=1
                )

            a = amps[t]
            inner += lax.dot_general(a * flat_row(weight), a, NT, precision=HIGHEST, preferred_element_type=F32)
            inner_rhs += lax.dot_general(
                jnp.broadcast_to(flat_row(pull), (8, LANES)), a, NT, precision=HIGHEST, preferred_element_type=F32
            )
        normal += inner * table_column * table_row
        rhs += inner_rhs * table_row
    factor = 1.0 / (FAM * MODES * TIPS)
    n_z[:, pl.ds(0, 2)] = (normal * factor).reshape(NZ, 2, 8, SECTORS)
    for i in range(NZ):
        n_z[i, 2] = rhs * factor

    for k in range(1, NZ):
        push("nz", n_z.at[z ^ k], n_from_z.at[z], me ^ (NXY * k), q)
    n_from_z[z] = n_z[z]
    arrived("nz", n_from_z.at[pl.ds(0, NZ - 1)])
    tiles = jnp.sum(n_from_z[...], axis=0)
    for i in range(2):
        n_xy[i, 0] = tiles[i]
        n_xy[i, 1] = tiles[2]
    for k in range(1, NXY):
        push("nxy", n_xy.at[(xy ^ k) // 4], n_from_xy.at[xy], me ^ k, q)
    n_from_xy[xy] = n_xy[xy // 4]
    arrived("nxy", n_from_xy.at[pl.ds(0, NXY - 1)])
    n_dof[q] = jnp.sum(n_from_xy[...], axis=0)
    for k in (1, 2, 3):
        push("ndof", n_dof.at[q], n_dof.at[q], me, q ^ k)
    arrived("ndof", n_dof.at[pl.ds(0, DOFS - 1)])
    tiles = jnp.sum(n_dof[...], axis=0)
    for l in range(2):
        normal_ref[pl.ds(l, 1), :] = jnp.sum(
            jnp.where(row == 2 * (xy % 4) + l, tiles[0], 0.0), axis=0, keepdims=True
        )
    pair_lane = lax.broadcasted_iota(jnp.int32, (1, 2), 1)
    ends = [
        jnp.sum(jnp.where((lane == 2 * me + l) & (row == 0), tiles[1], 0.0), axis=(0, 1), keepdims=True)
        for l in range(2)
    ]
    rhs_ref[...] = jnp.where(pair_lane == 0, ends[0], ends[1])

    arrived("mac", macs.at[pl.ds(0, DOFS - 1)])
    families = macs[...].reshape(FAM, LANES)
    mac_ref[0] = families[:, :MODES]
    mac_ref[1] = families[:, MODES:]

    for h in range(CHUNKS):
        arrived(f"out{h}", out_ref.at[:, pl.ds(ROWS * h, ROWS), pl.ds(0, LANES * (SEC - 1))])
        local = out_ref.at[:, pl.ds(ROWS * h, ROWS), pl.ds(0, LANES)]
        pltpu.make_async_copy(local, local, lsem.at[CHUNKS + h]).wait()
    for stage, ref in sent:
        total(stage, ref).wait_send()


def on_device(sector_modes, tip_modes, tip_index, nominal_eig, measured_eig, pairing):
    table, table_low, table_split, square_split, back = (jnp.asarray(a) for a in tables())
    vmem = pl.BlockSpec(memory_space=pltpu.VMEM)
    tile = (QF, LANES)
    harmonic, mac, normal, rhs = pl.pallas_call(
        body,
        out_shape=(
            jax.ShapeDtypeStruct(sector_modes.shape, BF16),
            jax.ShapeDtypeStruct((2, FAM, MODES), F32),
            jax.ShapeDtypeStruct((2, SECTORS), F32),
            jax.ShapeDtypeStruct((1, 2), F32),
        ),
        in_specs=[vmem] * 11,
        out_specs=(pl.BlockSpec(memory_space=pl.ANY), vmem, vmem, vmem),
        scratch_shapes=[
            pltpu.VMEM((CHUNKS, SECTORS, ROWS, LANES), BF16),
            pltpu.VMEM((SECTORS * ROWS, LANES), F32),
            pltpu.VMEM((SECTORS * ROWS, LANES), F32),
            pltpu.VMEM((CHUNKS, SECTORS, ROWS, LANES), BF16),
            pltpu.VMEM((2, NZ, NX, 2 * NY, MODES // 2, TIPS), BF16),
            pltpu.VMEM((SECTORS * HROWS, LANES), F32),
            pltpu.VMEM((SECTORS * MODES, LANES), F32),
            pltpu.VMEM((SECTORS, LANES), F32),
            pltpu.VMEM((DOFS, SEC + 1) + tile, F32),
            pltpu.VMEM((2, SEC + 1) + tile, F32),
            pltpu.VMEM((2, SEC + 1) + tile, F32),
            pltpu.VMEM((SEC + 1,) + tile, F32),
            pltpu.VMEM((NXY, NZ + 1) + tile, F32),
            pltpu.VMEM((NXY, NZ + 1) + tile, F32),
            pltpu.VMEM((NZ, 2) + tile, F32),
            pltpu.VMEM((NZ, 2) + tile, F32),
            pltpu.VMEM((NXY, NZ) + tile, F32),
            pltpu.VMEM((DOFS,) + tile, F32),
            pltpu.VMEM((NZ, 3, 8, SECTORS), F32),
            pltpu.VMEM((NZ, 3, 8, SECTORS), F32),
            pltpu.VMEM((2, 2, 8, SECTORS), F32),
            pltpu.VMEM((NXY, 2, 8, SECTORS), F32),
            pltpu.VMEM((DOFS, 2, 8, SECTORS), F32),
            pltpu.SemaphoreType.DMA((len(STAGES),)),
            pltpu.SemaphoreType.DMA((len(STAGES),)),
            pltpu.SemaphoreType.DMA((2 * CHUNKS,)),
        ],
        compiler_params=pltpu.CompilerParams(
            collective_id=0, has_side_effects=True, vmem_limit_bytes=48 * 2**20
        ),
        name="identify",
    )(
        sector_modes, tip_modes, tip_index, nominal_eig, measured_eig.reshape(1, MODES),
        pairing.reshape(1, MODES), table, table_low, table_split, square_split, back,
    )
    return harmonic, mac, normal, rhs.reshape(2)


def solution(mesh):
    return jax.shard_map(
        on_device,
        mesh=mesh,
        in_specs=(P("sec", None, "dof"), P("sec", None, None), P(), P("sec", None), P(), P()),
        out_specs=(P("sec", None, "dof"), P("sec", None, None), P("sec", None), P("sec")),
        check_vma=False,
    )
```

time: 1720 us -> 130 us (0.08)
  the two profiles are of different devices: /device:TPU:22 before, /device:TPU:1 now
where the time goes in v2:
time: 130 us; the launch traced here: 129 us
  Pallas kernels  118 us (91%)
  local copies, waits for them, and re-layouts  10.3 us (8%)
    pallas_call x1, Pallas kernels, on_device(): pl.pallas_call(body, out_shape=(jax.ShapeDtypeStruct(sector_modes.shape,...  118 us
    unnamed x26, local copies, waits for them, and re-layouts  10.3 us

profile of v2, /device:TPU:1, one launch (start us, length us, event | category | flops | bytes accessed | tf_op | source)
XLA Modules:
  0.0 129.1 jit_solution(10078861180559443226)
XLA Ops:
  0.6 0.0 copy-start.10
  0.6 0.0 copy-start.8
  0.7 0.0 copy-start.9
  0.7 0.6 copy-done.10
  1.3 0.0 copy-done.8
  1.3 0.0 copy-done.9
  1.3 0.0 copy-start
  1.3 1.2 copy-done
  2.6 0.0 copy-start.1
  2.6 0.9 copy-done.1
  3.5 0.0 copy-start.2
  3.5 0.8 copy-done.2
  4.3 0.0 copy-start.3
  4.3 0.8 copy-done.3
  5.1 0.0 copy-start.4
  5.1 0.8 copy-done.4
  6.0 0.8 copy-done.5
  6.8 0.8 copy-done.6
  7.6 0.8 copy-done.7
  8.3 118.1 %identify.1 = (bf16[2,32,8192]{2,1,0:T(8,128)(2,1)S(1)}, f32[2,32,64]{2,1,0:T(8,128)S(1)}, f32[2,128]{1,0:T(2,128)S(1)}, f32[1,2]{1,0:T(1,128)S(1)}) custom-call(bf16[2,32,8192]{2,1,0:T(8,128)(2,1)S(1)} %copy-done, bf16[2,64,128]{2,1,0:T(8,128)(2,1)S(1)} %copy-done.6, s32[128,128]{1,0:T(8,128)S(1)} %copy-done.2, f32[2,32]{1,0:T(2,128)S(1)} %copy-done.8, ...), custom_call_target="tpu_custom_call" | custom-call | tf_op jit(solution)/shard_map/identify/pallas_call | solution.py:349
  126.4 1.0 copy.19
  127.4 0.6 copy.20
  128.0 0.6 copy.21
  128.5 0.5 copy.22
  (3 shorter events, 0.0 us)
Async XLA Ops:
  0.6 0.7 copy-start.10
  0.6 0.7 copy-start.8
  0.7 0.7 copy-start.9
  1.3 1.2 copy-start
  2.6 0.9 copy-start.1
  3.5 0.8 copy-start.2
  4.3 0.8 copy-start.3
  5.1 0.8 copy-start.4
  6.0 0.8 copy-start.5
  6.8 0.8 copy-start.6
  7.6 0.8 copy-start.7

commit v3 on v2

v3 whole, which is shorter than its diff:
```python
import math

import jax
import jax.numpy as jnp
import numpy as np
from jax import lax
from jax.experimental import pallas as pl
from jax.experimental.pallas import tpu as pltpu
from jax.sharding import PartitionSpec as P

MESH = pl.DeviceIdType.MESH
HIGHEST = lax.Precision.HIGHEST
F32 = jnp.float32
BF16 = jnp.bfloat16
NT = (((1,), (1,)), ((), ()))

SECTORS, FAM, MODES, TIPS, LANES = 128, 32, 64, 128, 128
SEC, DOFS = 64, 4
NZ, NX, NY, NXY = 8, 4, 2, 8
CHUNKS = 2
ROWS = FAM // CHUNKS
HROWS = MODES + 8
QF = FAM // DOFS
PAIRS = SEC // 2 + 1
PIECES = 8
STAGES = (
    "in0", "in1", "out0", "out1", "tip_zy", "x1p", "x1m", "x2p", "x2m", "c0", "cm", "cp", "c2",
    "core", "xy", "z", "rows_xy", "rows",
)
STAGE = {name: i for i, name in enumerate(STAGES)}
LOCAL = ("in0", "in1", "out0", "out1", "tips", "index", "nominal", "low", "split", "square", "forth", "back")


def tables():
    rows, cols = np.meshgrid(np.arange(SECTORS), np.arange(SECTORS), indexing="ij")
    angle = 2.0 * np.pi * (rows * cols % SECTORS) / SECTORS
    table = math.sqrt(2.0 / SECTORS) * np.where(rows <= SECTORS // 2, np.cos(angle), np.sin(angle))
    table = table.astype(np.float32)

    def split(a):
        high = a.astype(BF16)
        low = (a - high.astype(np.float32)).astype(BF16)
        return np.concatenate([high, low], axis=1)

    forth = np.concatenate([table[0::2], table[1::2]], axis=0)
    back = np.concatenate([forth.T[0::2], forth.T[1::2]], axis=0)
    return table.astype(BF16), split(table), split(table * table), forth, back


def body(
    x_ref, tips_ref, index_hbm, nominal_hbm, measured_ref, pairing_ref,
    low_hbm, split_hbm, square_hbm, forth_hbm, back_hbm,
    out_ref, mac_ref, normal_ref, rhs_ref,
    index_ref, nominal_ref, low_ref, split_ref, square_ref, forth_ref, back_ref,
    recv, wide, done, mid, tips, spread, gather, gather_split, power, tip_power_ref,
    part, to_core, from_core, half, mine_xy, from_xy, mine_z, from_z, mine_sec, from_sec, mine_rows, from_rows,
    ssem, rsem, lsem,
):
    me, q = lax.axis_index("sec"), lax.axis_index("dof")
    z, x, y = me // NXY, (me // NY) % NX, me % NY
    xy = me % NXY
    lo, core = q // 2, q % 2
    quarter = 2 * core + lo

    barrier = pltpu.get_barrier_semaphore()

    def greet(k, c):
        pl.semaphore_signal(barrier, inc=1, device_id=(me ^ k, q), device_id_type=MESH)
        return c

    lax.fori_loop(1, SEC, greet, 0)
    for k in (1, 2, 3):
        pl.semaphore_signal(barrier, inc=1, device_id=(me, q ^ k), device_id_type=MESH)
    for k in range(1, NXY):
        pl.semaphore_signal(barrier, inc=1, device_id=(me ^ k, q ^ 2), device_id_type=MESH)
        for b in (1, 2, 3):
            pl.semaphore_signal(barrier, inc=1, device_id=(me ^ (NXY * k), q ^ b), device_id_type=MESH)

    def local(name, src, dst):
        return pltpu.make_async_copy(src, dst, lsem.at[LOCAL.index(name)])

    own_y = pl.ds(2 * y, 2)
    half_modes = pl.ds(pl.multiple_of(32 * core, 32), 32)
    own_tips = local("tips", tips_ref.at[:, half_modes, :], tips.at[core, z, x, own_y])
    own_tips.start()
    loads = [
        local(name, src, dst)
        for name, src, dst in (
            ("index", index_hbm, index_ref), ("nominal", nominal_hbm, nominal_ref), ("low", low_hbm, low_ref),
            ("split", split_hbm, split_ref), ("square", square_hbm, square_ref),
            ("forth", forth_hbm, forth_ref), ("back", back_hbm, back_ref),
        )
    ]
    for load in loads:
        load.start()

    def push(stage, src, dst, sec, dof):
        pltpu.make_async_remote_copy(
            src_ref=src, dst_ref=dst, send_sem=ssem.at[STAGE[stage]], recv_sem=rsem.at[STAGE[stage]],
            device_id=(sec, dof), device_id_type=MESH,
        ).start()

    def total(stage, ref):
        return pltpu.make_async_remote_copy(
            src_ref=ref, dst_ref=ref, send_sem=ssem.at[STAGE[stage]], recv_sem=rsem.at[STAGE[stage]],
            device_id=(me, q), device_id_type=MESH,
        )

    sent = []

    def arrived(stage, ref):
        with jax.named_scope("wait_" + stage):
            total(stage, ref).wait_recv()
        sent.append((stage, ref))

    def columns(j):
        return pl.ds(pl.multiple_of(LANES * j, LANES), LANES)

    def mine(j):
        return pl.ds(2 * j, 2)

    def send_in(h):
        family = pl.ds(ROWS * h, ROWS)

        def step(k, c):
            j = me ^ k
            push(f"in{h}", x_ref.at[:, family, columns(j)], recv.at[h, mine(me)], j, q)
            return c

        lax.fori_loop(1, SEC, step, 0)
        local(f"in{h}", x_ref.at[:, family, columns(me)], recv.at[h, mine(me)]).start()

    def transform(h):
        arrived(f"in{h}", recv.at[h, pl.ds(0, 2 * (SEC - 1))])
        local(f"in{h}", recv.at[h, mine(me)], recv.at[h, mine(me)]).wait()
        wide[...] = recv[h].reshape(SECTORS * ROWS, LANES).astype(F32)
        table = low_ref[...]
        for f in range(0, ROWS, 2):
            pair = [wide[pl.ds(f + i, SECTORS, stride=ROWS), :] for i in range(2)]
            both = jnp.concatenate(pair, axis=1).astype(BF16)
            result = jnp.dot(table, both, preferred_element_type=F32)
            for i in range(2):
                done[pl.ds(f + i, SECTORS, stride=ROWS), :] = result[:, LANES * i:LANES * (i + 1)]
        mid[h] = done[...].reshape(SECTORS, ROWS, LANES).astype(BF16)
        family = pl.ds(ROWS * h, ROWS)

        def step(k, c):
            j = me ^ k
            push(f"out{h}", mid.at[h, mine(j)], out_ref.at[:, family, columns(me)], j, q)
            return c

        lax.fori_loop(1, SEC, step, 0)
        local(f"out{h}", mid.at[h, mine(me)], out_ref.at[:, family, columns(me)]).start()

    first = q * (SEC * LANES) + me * LANES
    column_ids = first + lax.broadcasted_iota(jnp.int32, (LANES, TIPS), 0)
    ones = jnp.ones((16, TIPS), BF16)

    def spread_column(at, tip_sum):
        def step(k, tip_sum):
            for i in range(2 * NY):
                s = 2 * NXY * k + 2 * NY * at + i
                one = [tips[c, k, at, i] for c in range(2)]
                block = jnp.concatenate(one + [ones], axis=0)
                chosen = jnp.where(index_ref[pl.ds(s, 1), :] == column_ids, 1.0, 0.0).astype(BF16)
                result = lax.dot_general(block, chosen, NT, preferred_element_type=F32)
                spread[pl.ds(pl.multiple_of(s * HROWS, 8), HROWS), :] = result[:HROWS]
                both = jnp.concatenate(one, axis=0).astype(F32)
                tip_sum = tip_sum + both * both
            return tip_sum

        with jax.named_scope("spread"):
            return lax.fori_loop(0, NZ, step, tip_sum)

    with jax.named_scope("barrier"):
        pl.semaphore_wait(barrier, SEC + 30)
    own_tips.wait()

    own_block = tips.at[core, z, x, own_y]
    for k in range(1, NZ):
        push("tip_zy", own_block, own_block, me ^ (NXY * k), q)
    for k in range(NZ):
        push("tip_zy", own_block, own_block, me ^ (NXY * k + 1), q)
    send_in(0)
    send_in(1)
    for load in loads:
        load.wait()
    arrived("tip_zy", tips.at[core, pl.ds(0, 5), pl.ds(0, 3), pl.ds(0, 2)])
    xp, xm, xf = (x + 1) % NX, (x + 3) % NX, (x + 2) % NX
    right, left = me + NY * (xp - x), me + NY * (xm - x)
    push("x1p", tips.at[core, :, x], tips.at[core, :, x], right, q)
    push("x1m", tips.at[core, :, x], tips.at[core, :, x], left, q)
    push("c0", tips.at[core, :, x], tips.at[core, :, x], me, q ^ 1)
    arrived("c0", tips.at[core, :, x])
    tip_sum = spread_column(x, jnp.zeros((MODES, TIPS), F32))
    arrived("x1p", tips.at[core, :, xm])
    push("x2p", tips.at[core, :, xm, pl.ds(0, 2)], tips.at[core, :, xm, pl.ds(0, 2)], right, q)
    push("cm", tips.at[core, :, xm], tips.at[core, :, xm], me, q ^ 1)
    arrived("x1m", tips.at[core, :, xp])
    push("x2m", tips.at[core, :, xp, pl.ds(2, 2)], tips.at[core, :, xp, pl.ds(2, 2)], left, q)
    push("cp", tips.at[core, :, xp], tips.at[core, :, xp], me, q ^ 1)
    with jax.named_scope("transform0"):
        transform(0)
    arrived("cm", tips.at[core, :, xm])
    tip_sum = spread_column(xm, tip_sum)
    arrived("x2p", tips.at[core, :, xf, pl.ds(0, 2)])
    arrived("x2m", tips.at[core, :, xf, pl.ds(2, 2)])
    push("c2", tips.at[core, :, xf], tips.at[core, :, xf], me, q ^ 1)
    arrived("cp", tips.at[core, :, xp])
    tip_sum = spread_column(xp, tip_sum)
    arrived("c2", tips.at[core, :, xf])
    tip_sum = spread_column(xf, tip_sum)
    with jax.named_scope("transform1"):
        transform(1)

    def twice(a):
        low = a.astype(BF16)
        return jnp.concatenate([low, low], axis=0)

    with jax.named_scope("gather"):
        for m in range(0, MODES, 2):
            pair = [spread[pl.ds(m + i, SECTORS, stride=HROWS), :] for i in range(2)]
            both = twice(jnp.concatenate(pair, axis=1))
            result = jnp.dot(split_ref[...], both, preferred_element_type=F32)
            for i in range(2):
                gather[pl.ds(m + i, SECTORS, stride=MODES), :] = result[:, LANES * i:LANES * (i + 1)]
        counts = spread[pl.ds(MODES, SECTORS, stride=HROWS), :]
        power[...] = jnp.dot(square_ref[...], twice(counts), preferred_element_type=F32)

        def split_step(j, c):
            g = gather[pl.ds(pl.multiple_of(j * LANES, LANES), LANES), :]
            high = g.astype(BF16)
            gather_split[j] = jnp.concatenate([high, (g - high.astype(F32)).astype(BF16)], axis=1)
            return c

        lax.fori_loop(0, SEC, split_step, 0, unroll=2)
        tip_power_ref[...] = jnp.broadcast_to(jnp.sum(tip_sum, axis=1, keepdims=True), (MODES, LANES))


    lane_ids = lax.broadcasted_iota(jnp.int32, (FAM, LANES), 1)

    def project_step(j, mode_power):
        rows = jnp.concatenate([mid[h, 2 * j + l] for l in range(2) for h in range(CHUNKS)], axis=0)
        both = lax.dot_general(
            jnp.concatenate([rows, rows], axis=1), gather_split[j], NT, preferred_element_type=F32
        )
        pair = jnp.where(lane_ids < MODES, both[:FAM], both[FAM:])
        part[:, j] = pair.reshape(DOFS, QF, LANES)
        rows = rows.astype(F32)
        for l in range(2):
            one = rows[FAM * l:FAM * (l + 1)]
            share = jnp.sum(one * one * power[pl.ds(2 * j + l, 1), :], axis=1, keepdims=True)
            mode_power = jnp.where(lane_ids == SEC * l + j, share, mode_power)
        return mode_power

    with jax.named_scope("project"):
        mode_power = lax.fori_loop(0, SEC, project_step, jnp.zeros((FAM, LANES), F32), unroll=4)
        part[:, SEC] = mode_power.reshape(DOFS, QF, LANES)
        part[:, SEC + 1] = jnp.zeros((DOFS, QF, LANES), F32)

    to_core[...] = part[pl.ds(2 * (1 - core), 2)].reshape(2, PAIRS, 2 * QF, LANES).astype(BF16)
    push("core", to_core, from_core, me, q ^ 1)
    arrived("core", from_core)
    sums = part[pl.ds(2 * core, 2)] + from_core[...].astype(F32).reshape(2, 2 * PAIRS, QF, LANES)
    half[...] = sums.reshape(2 * 2 * PAIRS * QF, LANES)

    lane = lax.broadcasted_iota(jnp.int32, (8, LANES), 1)
    row = lax.broadcasted_iota(jnp.int32, (8, LANES), 0)
    family_row = lax.broadcasted_iota(jnp.int32, (QF, FAM), 0)
    family_lane = lax.broadcasted_iota(jnp.int32, (QF, FAM), 1)
    with jax.named_scope("turn"):
        for i in range(2):
            at = 2 * PAIRS * QF * i
            turned = []
            for f in range(QF):
                one = half[pl.ds(at + f, SEC, stride=QF), :].T
                one = jnp.concatenate([one[:MODES], one[MODES:]], axis=1)
                turned.append(one.reshape(NXY, 8, LANES))
            for f in range(0, QF, 2):
                mine_xy[NXY * i:NXY * (i + 1), f // 2] = jnp.concatenate(turned[f:f + 2], axis=1).astype(BF16)
            nominal = jnp.zeros((QF, LANES), F32)
            for l in range(2):
                own = jnp.where(
                    family_row + QF * (2 * core + i) == family_lane, nominal_ref[pl.ds(l, 1), :], 0.0
                )
                own = jnp.sum(own, axis=1, keepdims=True)
                nominal = jnp.where((lane == SEC * l + me) & (lo == i), own, nominal)
            high = nominal.astype(BF16)
            rest = nominal - high.astype(F32)
            middle = rest.astype(BF16)
            last = (rest - middle.astype(F32)).astype(BF16)
            power_tile = half[pl.ds(at + SEC * QF, QF), :].astype(BF16)
            for k in range(NXY):
                mine_xy[NXY * i + k, 4] = jnp.concatenate([power_tile, high], axis=0)
                mine_xy[NXY * i + k, 5] = jnp.concatenate([middle, last], axis=0)
    slot = NXY * lo + xy
    for b in range(2):
        for k in range(1 - b, NXY):
            push("xy", mine_xy.at[NXY * (lo ^ b) + (xy ^ k)], from_xy.at[slot], me ^ k, q ^ (2 * b))
    from_xy[slot] = mine_xy[slot]
    arrived("xy", from_xy.at[pl.ds(0, 2 * NXY - 1)])
    column = jnp.sum(from_xy[...].astype(F32), axis=0)
    families = column[:4].reshape(QF, 8, LANES)
    power_tile, nominal = column[4, :8], column[4, 8:] + column[5, :8] + column[5, 8:]
    mine_z[:, 0] = families
    for i in range(NZ):
        mine_z[i, 1] = power_tile
        mine_z[i, 2] = nominal
    for k in range(1, NZ):
        push("z", mine_z.at[z ^ k], from_z.at[z], me ^ (NXY * k), q)
    from_z[z] = mine_z[z]
    arrived("z", from_z.at[pl.ds(0, NZ - 1)])
    whole = jnp.sum(from_z[...], axis=0)

    with jax.named_scope("normal"):
        projection = whole[0]
        mode_power, nominal = (
            jnp.sum(jnp.where(row == z, whole[i], 0.0), axis=0, keepdims=True) for i in (1, 2)
        )
        tip_power = tip_power_ref[pl.ds(pl.multiple_of(8 * xy, 8), 8), :]
        mac = (SECTORS * TIPS) * projection * projection / ((mode_power + 1e-06) * (tip_power + 1e-06))
        own_mode = lax.broadcasted_iota(jnp.int32, (8, MODES), 1) == 8 * xy + lax.broadcasted_iota(
            jnp.int32, (8, MODES), 0
        )
        pairing = jnp.sum(jnp.where(own_mode, pairing_ref[...].astype(F32), 0.0), axis=1, keepdims=True)
        measured = jnp.sum(jnp.where(own_mode, measured_ref[...], 0.0), axis=1, keepdims=True)
        family = (QF * quarter + z).astype(F32)
        weight = mac + jnp.where(pairing == family, 4.0, 0.0)
        pull = weight * ((measured - nominal) * projection)
        mac_rows = lax.dot_general(
            mac, jnp.where(own_mode, 1.0, 0.0), (((0,), (0,)), ((), ())),
            precision=HIGHEST, preferred_element_type=F32,
        )

        forth, back = forth_ref[...], back_ref[...]
        amps = jnp.dot(projection, forth, precision=HIGHEST, preferred_element_type=F32)
        amps_column = lax.dot_general(back, projection, NT, precision=HIGHEST, preferred_element_type=F32)
        left = jnp.concatenate([back * weight[k:k + 1, :] for k in range(8)], axis=0)
        pairs = jnp.dot(left, forth, precision=HIGHEST, preferred_element_type=F32)
        normal = jnp.zeros((SECTORS, SECTORS), F32)
        for k in range(8):
            normal += amps_column[:, k:k + 1] * (amps[k:k + 1, :] * pairs[SECTORS * k:SECTORS * (k + 1)])
        pulled = jnp.dot(pull, forth, precision=HIGHEST, preferred_element_type=F32)
        rhs = jnp.sum(amps * pulled, axis=0, keepdims=True)
        factor = 1.0 / (FAM * MODES * TIPS)
        normal = normal * factor
        rows = (
            normal[:SEC], normal[SEC:], jnp.broadcast_to(rhs * factor, (SEC, SECTORS)),
            jnp.concatenate([mac_rows[:SEC], mac_rows[SEC:]], axis=1),
        )
        for i in range(4):
            mine_sec[:, :, i, :] = rows[i].reshape(NZ, NXY, SECTORS)

    for k in range(1, NXY):
        push("rows_xy", mine_sec.at[:, xy ^ k], from_sec.at[xy], me ^ k, q)
    from_sec[xy] = mine_sec[:, xy]
    arrived("rows_xy", from_sec.at[pl.ds(0, NXY - 1)])
    mine_rows[...] = jnp.sum(from_sec[...], axis=0)
    slot = NZ * q + z
    for b in range(DOFS):
        for k in range(0 if b else 1, NZ):
            push("rows", mine_rows.at[z ^ k], from_rows.at[slot], me ^ (NXY * k), q ^ b)
    from_rows[slot] = mine_rows[z]
    arrived("rows", from_rows.at[pl.ds(0, DOFS * NZ - 1)])
    rows = jnp.sum(from_rows[...], axis=0)
    normal_ref[...] = rows[:2]
    pair_lane = lax.broadcasted_iota(jnp.int32, (1, 2), 1)
    rhs_lane = lax.broadcasted_iota(jnp.int32, (1, LANES), 1)
    ends = [
        jnp.sum(jnp.where(rhs_lane == 2 * me + l, rows[2:3], 0.0), axis=1, keepdims=True) for l in range(2)
    ]
    rhs_ref[...] = jnp.where(pair_lane == 0, ends[0], ends[1])
    for i in range(DOFS):
        tile = from_rows[NZ * i:NZ * (i + 1), 3, :]
        for l in range(2):
            mac_ref[l, pl.ds(QF * (2 * (i % 2) + i // 2), QF), :] = tile[:, MODES * l:MODES * (l + 1)]

    for h in range(CHUNKS):
        arrived(f"out{h}", out_ref.at[:, pl.ds(ROWS * h, ROWS), pl.ds(0, LANES * (SEC - 1))])
        own = out_ref.at[:, pl.ds(ROWS * h, ROWS), pl.ds(0, LANES)]
        local(f"out{h}", own, own).wait()
    for stage, ref in sent:
        total(stage, ref).wait_send()


def write(long_ref, *refs):
    short, long_out, short_out = refs[:3], refs[3], refs[4:7]
    held, short_sems, in_sems, out_sems = refs[7:]
    count, width = held.shape[0], held.shape[-1]
    parts = [pl.ds(width * i, width) for i in range(count)]
    copies = [pltpu.make_async_copy(long_ref.at[:, :, parts[i]], held.at[i], in_sems.at[i]) for i in range(count)]
    for copy in copies:
        copy.start()
    ends = [pltpu.make_async_copy(short[i], short_out[i], short_sems.at[i]) for i in range(3)]
    for end in ends:
        end.start()
    for i in range(count):
        copies[i].wait()
        end = pltpu.make_async_copy(held.at[i], long_out.at[:, :, parts[i]], out_sems.at[i])
        end.start()
        ends.append(end)
    for end in ends:
        end.wait()


def on_device(sector_modes, tip_modes, tip_index, nominal_eig, measured_eig, pairing):
    constants = [jnp.asarray(a) for a in tables()]
    vmem = pl.BlockSpec(memory_space=pltpu.VMEM)
    hbm = pl.BlockSpec(memory_space=pltpu.HBM)
    tile = (QF, LANES)
    results = pl.pallas_call(
        body,
        out_shape=(
            jax.ShapeDtypeStruct(sector_modes.shape, BF16),
            jax.ShapeDtypeStruct((2, FAM, MODES), F32),
            jax.ShapeDtypeStruct((2, SECTORS), F32),
            jax.ShapeDtypeStruct((1, 2), F32),
        ),
        in_specs=[hbm] * 4 + [vmem] * 2 + [hbm] * 5,
        out_specs=(hbm, vmem, vmem, vmem),
        scratch_shapes=[
            pltpu.VMEM((SECTORS, TIPS), jnp.int32),
            pltpu.VMEM((2, FAM), F32),
            pltpu.VMEM((SECTORS, SECTORS), BF16),
            pltpu.VMEM((SECTORS, 2 * SECTORS), BF16),
            pltpu.VMEM((SECTORS, 2 * SECTORS), BF16),
            pltpu.VMEM((SECTORS, SECTORS), F32),
            pltpu.VMEM((SECTORS, SECTORS), F32),
            pltpu.VMEM((CHUNKS, SECTORS, ROWS, LANES), BF16),
            pltpu.VMEM((SECTORS * ROWS, LANES), F32),
            pltpu.VMEM((SECTORS * ROWS, LANES), F32),
            pltpu.VMEM((CHUNKS, SECTORS, ROWS, LANES), BF16),
            pltpu.VMEM((2, NZ, NX, 2 * NY, MODES // 2, TIPS), BF16),
            pltpu.VMEM((SECTORS * HROWS, LANES), F32),
            pltpu.VMEM((SECTORS * MODES, LANES), F32),
            pltpu.VMEM((SEC, LANES, 2 * LANES), BF16),
            pltpu.VMEM((SECTORS, LANES), F32),
            pltpu.VMEM((MODES, LANES), F32),
            pltpu.VMEM((DOFS, 2 * PAIRS) + tile, F32),
            pltpu.VMEM((2, PAIRS, 2 * QF, LANES), BF16),
            pltpu.VMEM((2, PAIRS, 2 * QF, LANES), BF16),
            pltpu.VMEM((2 * 2 * PAIRS * QF, LANES), F32),
            pltpu.VMEM((2 * NXY, 6, 16, LANES), BF16),
            pltpu.VMEM((2 * NXY, 6, 16, LANES), BF16),
            pltpu.VMEM((NZ, 3) + tile, F32),
            pltpu.VMEM((NZ, 3) + tile, F32),
            pltpu.VMEM((NZ, NXY, 4, LANES), F32),
            pltpu.VMEM((NXY, NZ, 4, LANES), F32),
            pltpu.VMEM((NZ, 4, LANES), F32),
            pltpu.VMEM((DOFS * NZ, 4, LANES), F32),
            pltpu.SemaphoreType.DMA((len(STAGES),)),
            pltpu.SemaphoreType.DMA((len(STAGES),)),
            pltpu.SemaphoreType.DMA((len(LOCAL),)),
        ],
        compiler_params=pltpu.CompilerParams(
            collective_id=0, has_side_effects=True, vmem_limit_bytes=60 * 2**20
        ),
        name="identify",
    )(
        sector_modes, tip_modes, tip_index, nominal_eig, measured_eig.reshape(1, MODES),
        pairing.reshape(1, MODES), *constants,
    )
    harmonic, mac, normal, rhs = pl.pallas_call(
        write,
        out_shape=[jax.ShapeDtypeStruct(a.shape, a.dtype) for a in results],
        in_specs=[hbm] + [vmem] * 3,
        out_specs=[hbm] * 4,
        scratch_shapes=[
            pltpu.VMEM((PIECES, 2, FAM, sector_modes.shape[2] // PIECES), BF16),
            pltpu.SemaphoreType.DMA((3,)),
            pltpu.SemaphoreType.DMA((PIECES,)),
            pltpu.SemaphoreType.DMA((PIECES,)),
        ],
        name="write",
    )(*results)
    return harmonic, mac, normal, rhs.reshape(2)


def solution(mesh):
    return jax.shard_map(
        on_device,
        mesh=mesh,
        in_specs=(P("sec", None, "dof"), P("sec", None, None), P(), P("sec", None), P(), P()),
        out_specs=(P("sec", None, "dof"), P("sec", None, None), P("sec", None), P("sec")),
        check_vma=False,
    )
```

time: 130 us -> 90.7 us (0.70)
  Pallas kernels: 118 us -> 89.9 us
  local copies, waits for them, and re-layouts: 10.3 us -> 0 us
    pallas_call x1, Pallas kernels: 118 us -> 87 us  [on_device(): pl.pallas_call(body, out_shape=(jax.ShapeDtypeStruct(sector_modes.shape,...]
    unnamed x26 -> x0, local copies, waits for them, and re-layouts: 10.3 us -> none
    pallas_call x0 -> x1, Pallas kernels: none -> 2.89 us  [on_device(): pl.pallas_call(write, out_shape=[jax.ShapeDtypeStruct(a.shape, a.dtype) f...]
where the time goes in v3:
time: 90.7 us; the launch traced here: 90.5 us
  Pallas kernels  89.9 us (99%)
    pallas_call x1, Pallas kernels, on_device(): pl.pallas_call(body, out_shape=(jax.ShapeDtypeStruct(sector_modes.shape,...  87 us
    pallas_call x1, Pallas kernels, on_device(): pl.pallas_call(write, out_shape=[jax.ShapeDtypeStruct(a.shape, a.dtype) f...  2.89 us

profile of v3, /device:TPU:1, one launch (start us, length us, event | category | flops | bytes accessed | tf_op | source)
XLA Modules:
  0.0 90.5 jit_solution(230396815752030556)
XLA Ops:
  0.6 87.0 %identify.1 = (bf16[2,32,8192]{2,1,0:T(8,128)(2,1)}, f32[2,32,64]{2,1,0:T(8,128)}, f32[2,128]{1,0:T(2,128)}, f32[1,2]{1,0:T(1,128)}) custom-call(bf16[2,32,8192]{2,1,0:T(8,128)(2,1)} %x_ref.1, bf16[2,64,128]{2,1,0:T(8,128)(2,1)} %tips_ref.1, s32[128,128]{1,0:T(8,128)} %index_hbm.1, f32[2,32]{1,0:T(2,128)} %nominal_hbm.1, f32[1,64]{1,0:T(1,128)} %bitcast.3, ...), custom_call_target="tpu_custom_call" | custom-call | tf_op jit(solution)/shard_map/identify/pallas_call | solution.py:411
  87.6 2.9 %write.1 = (bf16[2,32,8192]{2,1,0:T(8,128)(2,1)}, f32[2,32,64]{2,1,0:T(8,128)}, f32[2,128]{1,0:T(2,128)}, f32[1,2]{1,0:T(1,128)}) custom-call(bf16[2,32,8192]{2,1,0:T(8,128)(2,1)} %get-tuple-element.12.long_ref, f32[2,32,64]{2,1,0:T(8,128)} %get-tuple-element.13.refs_0_, f32[2,128]{1,0:T(2,128)} %get-tuple-element.14.refs_1_, f32[1,2]{1,0:T(1,128)} %get-tuple-element.15.refs_2_), custom_call_target="tpu_custom_call" | custom-call | tf_op jit(solution)/shard_map/write/pallas_call | solution.py:463

commit v4 on v3

--- a/solution.py
+++ b/solution.py
@@ -22,13 +22,12 @@
 HROWS = MODES + 8
 QF = FAM // DOFS
 PAIRS = SEC // 2 + 1
-PIECES = 8
 STAGES = (
     "in0", "in1", "out0", "out1", "tip_zy", "x1p", "x1m", "x2p", "x2m", "c0", "cm", "cp", "c2",
     "core", "xy", "z", "rows_xy", "rows",
 )
 STAGE = {name: i for i, name in enumerate(STAGES)}
-LOCAL = ("in0", "in1", "out0", "out1", "tips", "index", "nominal", "low", "split", "square", "forth", "back")
+LOCAL = ("in0", "in1", "out0", "out1", "tips", "index", "nominal", "measured", "pairing", "low", "split", "square", "forth", "back")
 
 
 def tables():
@@ -48,10 +47,10 @@
 
 
 def body(
-    x_ref, tips_ref, index_hbm, nominal_hbm, measured_ref, pairing_ref,
+    x_ref, tips_ref, index_hbm, nominal_hbm, measured_hbm, pairing_hbm,
     low_hbm, split_hbm, square_hbm, forth_hbm, back_hbm,
     out_ref, mac_ref, normal_ref, rhs_ref,
-    index_ref, nominal_ref, low_ref, split_ref, square_ref, forth_ref, back_ref,
+    index_ref, nominal_ref, measured_ref, pairing_ref, low_ref, split_ref, square_ref, forth_ref, back_ref,
     recv, wide, done, mid, tips, spread, gather, gather_split, power, tip_power_ref,
     part, to_core, from_core, half, mine_xy, from_xy, mine_z, from_z, mine_sec, from_sec, mine_rows, from_rows,
     ssem, rsem, lsem,
@@ -86,7 +85,8 @@
     loads = [
         local(name, src, dst)
         for name, src, dst in (
-            ("index", index_hbm, index_ref), ("nominal", nominal_hbm, nominal_ref), ("low", low_hbm, low_ref),
+            ("index", index_hbm, index_ref), ("nominal", nominal_hbm, nominal_ref),
+            ("measured", measured_hbm, measured_ref), ("pairing", pairing_hbm, pairing_ref), ("low", low_hbm, low_ref),
             ("split", split_hbm, split_ref), ("square", square_hbm, square_ref),
             ("forth", forth_hbm, forth_ref), ("back", back_hbm, back_ref),
         )
@@ -142,6 +142,8 @@
             for i in range(2):
                 done[pl.ds(f + i, SECTORS, stride=ROWS), :] = result[:, LANES * i:LANES * (i + 1)]
         mid[h] = done[...].reshape(SECTORS, ROWS, LANES).astype(BF16)
+
+    def send_out(h, low, high):
         family = pl.ds(ROWS * h, ROWS)
 
         def step(k, c):
@@ -149,8 +151,9 @@
             push(f"out{h}", mid.at[h, mine(j)], out_ref.at[:, family, columns(me)], j, q)
             return c
 
-        lax.fori_loop(1, SEC, step, 0)
-        local(f"out{h}", mid.at[h, mine(me)], out_ref.at[:, family, columns(me)]).start()
+        lax.fori_loop(low, high, step, 0)
+        if low == 1:
+            local(f"out{h}", mid.at[h, mine(me)], out_ref.at[:, family, columns(me)]).start()
 
     first = q * (SEC * LANES) + me * LANES
     column_ids = first + lax.broadcasted_iota(jnp.int32, (LANES, TIPS), 0)
@@ -201,6 +204,7 @@
     push("cp", tips.at[core, :, xp], tips.at[core, :, xp], me, q ^ 1)
     with jax.named_scope("transform0"):
         transform(0)
+        send_out(0, 1, SEC)
     arrived("cm", tips.at[core, :, xm])
     tip_sum = spread_column(xm, tip_sum)
     arrived("x2p", tips.at[core, :, xf, pl.ds(0, 2)])
@@ -210,8 +214,6 @@
     tip_sum = spread_column(xp, tip_sum)
     arrived("c2", tips.at[core, :, xf])
     tip_sum = spread_column(xf, tip_sum)
-    with jax.named_scope("transform1"):
-        transform(1)
 
     def twice(a):
         low = a.astype(BF16)
@@ -236,6 +238,10 @@
         lax.fori_loop(0, SEC, split_step, 0, unroll=2)
         tip_power_ref[...] = jnp.broadcast_to(jnp.sum(tip_sum, axis=1, keepdims=True), (MODES, LANES))
 
+
+    with jax.named_scope("transform1"):
+        transform(1)
+    send_out(1, 1, 30)
 
     lane_ids = lax.broadcasted_iota(jnp.int32, (FAM, LANES), 1)
 
@@ -297,6 +303,7 @@
     for b in range(2):
         for k in range(1 - b, NXY):
             push("xy", mine_xy.at[NXY * (lo ^ b) + (xy ^ k)], from_xy.at[slot], me ^ k, q ^ (2 * b))
+    send_out(1, 30, 42)
     from_xy[slot] = mine_xy[slot]
     arrived("xy", from_xy.at[pl.ds(0, 2 * NXY - 1)])
     column = jnp.sum(from_xy[...].astype(F32), axis=0)
@@ -308,6 +315,7 @@
         mine_z[i, 2] = nominal
     for k in range(1, NZ):
         push("z", mine_z.at[z ^ k], from_z.at[z], me ^ (NXY * k), q)
+    send_out(1, 42, 54)
     from_z[z] = mine_z[z]
     arrived("z", from_z.at[pl.ds(0, NZ - 1)])
     whole = jnp.sum(from_z[...], axis=0)
@@ -353,6 +361,7 @@
 
     for k in range(1, NXY):
         push("rows_xy", mine_sec.at[:, xy ^ k], from_sec.at[xy], me ^ k, q)
+    send_out(1, 54, SEC)
     from_sec[xy] = mine_sec[:, xy]
     arrived("rows_xy", from_sec.at[pl.ds(0, NXY - 1)])
     mine_rows[...] = jnp.sum(from_sec[...], axis=0)
@@ -383,24 +392,13 @@
         total(stage, ref).wait_send()
 
 
-def write(long_ref, *refs):
-    short, long_out, short_out = refs[:3], refs[3], refs[4:7]
-    held, short_sems, in_sems, out_sems = refs[7:]
-    count, width = held.shape[0], held.shape[-1]
-    parts = [pl.ds(width * i, width) for i in range(count)]
-    copies = [pltpu.make_async_copy(long_ref.at[:, :, parts[i]], held.at[i], in_sems.at[i]) for i in range(count)]
+def write(*refs):
+    count = len(refs) // 2
+    copies = [pltpu.make_async_copy(refs[i], refs[count + i], refs[-1].at[i]) for i in range(count)]
     for copy in copies:
         copy.start()
-    ends = [pltpu.make_async_copy(short[i], short_out[i], short_sems.at[i]) for i in range(3)]
-    for end in ends:
-        end.start()
-    for i in range(count):
-        copies[i].wait()
-        end = pltpu.make_async_copy(held.at[i], long_out.at[:, :, parts[i]], out_sems.at[i])
-        end.start()
-        ends.append(end)
-    for end in ends:
-        end.wait()
+    for copy in copies:
+        copy.wait()
 
 
 def on_device(sector_modes, tip_modes, tip_index, nominal_eig, measured_eig, pairing):
@@ -416,11 +414,13 @@
             jax.ShapeDtypeStruct((2, SECTORS), F32),
             jax.ShapeDtypeStruct((1, 2), F32),
         ),
-        in_specs=[hbm] * 4 + [vmem] * 2 + [hbm] * 5,
-        out_specs=(hbm, vmem, vmem, vmem),
+        in_specs=[hbm] * 11,
+        out_specs=(pl.BlockSpec(memory_space=pl.ANY), vmem, vmem, vmem),
         scratch_shapes=[
             pltpu.VMEM((SECTORS, TIPS), jnp.int32),
             pltpu.VMEM((2, FAM), F32),
+            pltpu.VMEM((1, MODES), F32),
+            pltpu.VMEM((1, MODES), jnp.int32),
             pltpu.VMEM((SECTORS, SECTORS), BF16),
             pltpu.VMEM((SECTORS, 2 * SECTORS), BF16),
             pltpu.VMEM((SECTORS, 2 * SECTORS), BF16),
@@ -453,26 +453,28 @@
             pltpu.SemaphoreType.DMA((len(LOCAL),)),
         ],
         compiler_params=pltpu.CompilerParams(
-            collective_id=0, has_side_effects=True, vmem_limit_bytes=60 * 2**20
+            collective_id=0, has_side_effects=True, vmem_limit_bytes=40 * 2**20
         ),
         name="identify",
     )(
-        sector_modes, tip_modes, tip_index, nominal_eig, measured_eig.reshape(1, MODES),
-        pairing.reshape(1, MODES), *constants,
+        *[
+            pltpu.with_memory_space_constraint(a, pltpu.HBM)
+            for a in (
+                sector_modes, tip_modes, tip_index, nominal_eig, measured_eig.reshape(1, MODES),
+                pairing.reshape(1, MODES), *constants,
+            )
+        ]
     )
     harmonic, mac, normal, rhs = pl.pallas_call(
         write,
         out_shape=[jax.ShapeDtypeStruct(a.shape, a.dtype) for a in results],
-        in_specs=[hbm] + [vmem] * 3,
+        in_specs=[vmem] * 4,
         out_specs=[hbm] * 4,
         scratch_shapes=[
-            pltpu.VMEM((PIECES, 2, FAM, sector_modes.shape[2] // PIECES), BF16),
-            pltpu.SemaphoreType.DMA((3,)),
-            pltpu.SemaphoreType.DMA((PIECES,)),
-            pltpu.SemaphoreType.DMA((PIECES,)),
+            pltpu.SemaphoreType.DMA((4,)),
         ],
         name="write",
-    )(*results)
+    )(*[pltpu.with_memory_space_constraint(a, pltpu.VMEM) for a in results])
     return harmonic, mac, normal, rhs.reshape(2)
 
 

time: 90.7 us -> 85.7 us (0.945)
  Pallas kernels: 89.9 us -> 85 us
    pallas_call x1, Pallas kernels: 87 us -> 84 us  [on_device(): pl.pallas_call(body, out_shape=(jax.ShapeDtypeStruct(sector_modes.shape,...]
    pallas_call x1, Pallas kernels: 2.89 us -> 1.01 us  [on_device(): pl.pallas_call(write, out_shape=[jax.ShapeDtypeStruct(a.shape, a.dtype) f...]
where the time goes in v4:
time: 85.7 us
  Pallas kernels  85 us (99%)
    pallas_call x1, Pallas kernels, on_device(): pl.pallas_call(body, out_shape=(jax.ShapeDtypeStruct(sector_modes.shape,...  84 us

profile of v4, /device:TPU:1, one launch (start us, length us, event | category | flops | bytes accessed | tf_op | source)
XLA Modules:
  0.0 85.7 jit_solution(12354536715667492812)
XLA Ops:
  0.6 84.0 %identify.1 = (bf16[2,32,8192]{2,1,0:T(8,128)(2,1)S(1)}, f32[2,32,64]{2,1,0:T(8,128)S(1)}, f32[2,128]{1,0:T(2,128)S(1)}, f32[1,2]{1,0:T(1,128)S(1)}) custom-call(bf16[2,32,8192]{2,1,0:T(8,128)(2,1)} %x_ref.1, bf16[2,64,128]{2,1,0:T(8,128)(2,1)} %tips_ref.1, s32[128,128]{1,0:T(8,128)} %index_hbm.1, f32[2,32]{1,0:T(2,128)} %nominal_hbm.1, f32[1,64]{1,0:T(1,128)} %bitcast.3, ...), custom_call_target="tpu_custom_call" | custom-call | tf_op jit(solution)/shard_map/identify/pallas_call | solution.py:409
  84.7 1.0 %write.1 = (bf16[2,32,8192]{2,1,0:T(8,128)(2,1)}, f32[2,32,64]{2,1,0:T(8,128)}, f32[2,128]{1,0:T(2,128)}, f32[1,2]{1,0:T(1,128)}) custom-call(bf16[2,32,8192]{2,1,0:T(8,128)(2,1)S(1)} %get-tuple-element.12.refs_0_, f32[2,32,64]{2,1,0:T(8,128)S(1)} %get-tuple-element.13.refs_1_, f32[2,128]{1,0:T(2,128)S(1)} %get-tuple-element.14.refs_2_, ...), custom_call_target="tpu_custom_call" | custom-call | tf_op jit(solution)/shard_map/write/pallas_call | solution.py:468
